TPU v7x, 256 devices: a whole 4x4x8 slice. The times are simulated.
256 devices in a mesh: row: 16 (over z_hi, y), col: 4 (over z_lo, core), depth: 4 (over x).
Axes of the slice: x: 4, y: 4, z: 8 (z_hi: 4, z_lo: 2; z = z_hi * 2 + z_lo), core: 2. Of those that a mesh axis runs over, the one named last changes fastest.
Arguments:
- integrals: float32 [32768, 4096], P(('row', 'col'), 'depth'), may hold values from -0.09375 to 0.09375
- amplitudes: float32 [4096, 64, 64], P('depth', 'col', 'row'), may hold values from -6 to 6
Outputs:
- relaid: float32 [64, 64, 32768], P(('col', 'depth'), 'row')
All inputs are finite; a program needn't handle non-finite values.
Results may differ from a plain program's by a relative error of at most 0.00007.
Values sent between devices are 32-bit elements; how exact they have to be, the bound alone decides.
No kernel may reach another device: no remote copies, remote signals or barrier semaphores. Data moves between devices by JAX's collectives and lax.ppermute only.
A program may use at most 64 MiB of HBM per device.

v0:
```python
import jax
import jax.numpy as jnp
from jax import lax
from jax.sharding import PartitionSpec as P


def shards(integrals, amplitudes):
    rows_w = lax.all_gather(integrals, "col", axis=0, tiled=True)
    panel_t = lax.all_gather(amplitudes, "row", axis=2, tiled=True)
    kc_rows, i_count, j_count = panel_t.shape
    flat_panel = panel_t.reshape(kc_rows, i_count * j_count)
    row_count = lax.axis_size("row")
    ab_rows = rows_w.shape[0]
    summed = lax.psum_scatter(
        lax.dot_general(
            flat_panel,
            rows_w,
            (((0,), (1,)), ((), ())),
            precision=lax.Precision.HIGHEST,
            preferred_element_type=jnp.float32,
        ),
        "depth",
        scatter_dimension=0,
        tiled=True,
    )
    shares = summed.reshape(-1, j_count // row_count, row_count, ab_rows)
    exchanged = lax.all_to_all(shares, "row", split_axis=2, concat_axis=3, tiled=True)
    result = exchanged.reshape(shares.shape[0], j_count // row_count, row_count * ab_rows)
    return result


def solution(mesh):
    placed = (P(("row", "col"), "depth"), P("depth", "col", "row"))
    return jax.shard_map(
        shards,
        mesh=mesh,
        in_specs=placed,
        out_specs=P(("col", "depth"), "row", None),
        check_vma=False,
    )
```

profile of v0, /device:TPU:1, one launch (start us, length us, event | category | flops | bytes accessed | tf_op | source)
XLA Modules:
  0.0 360.2 jit_solution(4689598038092722052)
XLA Ops:
  6.5 0.0 all-gather.3.cloned.1.call-start
  6.5 1.8 copy.5
  8.3 0.0 all-gather.3.cloned.1.call-update
  8.4 0.0 all-gather.5.cloned.1.call-start
  8.4 0.7 all-gather.5.cloned.1.call-update
  9.1 0.0 reduce-scatter.2.cloned.1.call-start
  9.2 79.2 %all-gather.3.cloned.1.call-done = f32[1024,16,64]{0,1,2:T(8,128)} async-done(((f32[1024,16,4]{0,1,2:T(8,128)}), f32[1024,16,64]{0,1,2:T(8,128)}) %all-gather.3.cloned.1.call-update) | async-done | bytes 4194320 | tf_op jit(solution)/shard_map/all_gather | solution.py:9
  88.3 6.6 %copy.6 = f32[1024,16,64]{0,2,1:T(8,128)} copy(f32[1024,16,64]{0,1,2:T(8,128)} %all-gather.3.cloned.1.call-done) | data formatting | bytes 8388608 | tf_op jit(solution)/shard_map/all_gather | solution.py:9
  94.9 80.8 %all-gather.5.cloned.1.call-done = f32[2048,1024]{1,0:T(8,128)} async-done(((f32[512,1024]{1,0:T(8,128)}), f32[2048,1024]{1,0:T(8,128)}) %all-gather.5.cloned.1.call-update) | async-done | bytes 8388624 | tf_op jit(solution)/shard_map/all_gather | solution.py:8
  175.7 31.0 %fusion = f32[1024,2048]{1,0:T(8,128)} fusion(f32[1024,1024]{0,1:T(8,128)} %bitcast.7, f32[2048,1024]{1,0:T(8,128)} %all-gather.5.cloned.1.call-done), kind=kOutput, calls=%fused_computation | convolution fusion | flops 25769803776 | bytes 20971520 | tf_op jit(solution)/shard_map/dot_general | solution.py:15
  206.6 0.0 reduce-scatter.2.cloned.1.call-update
  206.7 83.1 %reduce-scatter.2.cloned.1.call-done = f32[256,2048]{1,0:T(8,128)} async-done(((f32[1024,2048]{1,0:T(8,128)}), f32[256,2048]{1,0:T(8,128)}) %reduce-scatter.2.cloned.1.call-update) | async-done | bytes 2097168 | tf_op jit(solution)/shard_map/reduce_scatter | solution.py:14
  289.8 2.9 copy.7
  292.7 59.5 %all_to_all.4 = f32[4,4,16,2048]{3,1,0,2:T(4,128)S(1)} all-to-all(f32[4,4,16,2048]{3,1,0,2:T(4,128)S(1)} %copy.7), channel_id=1, replica_groups=mesh['row'=16,'col'=4,'depth'=4] {'row'}, dimensions={2} | all-to-all | bytes 4194304 | tf_op jit(solution)/shard_map/all_to_all | solution.py:27
  352.3 1.5 copy.9
Async XLA Ops:
  6.5 81.8 %all-gather.3.cloned.1.call-start = ((), (), s32[]{:S(2)}) async-start(), calls=%async_computation.2 | async-start | bytes 4456448 | tf_op jit(solution)/shard_map/all_gather | solution.py:9
  8.4 167.3 %all-gather.5.cloned.1.call-start = ((), (), s32[]{:S(2)}) async-start(), calls=%async_computation.3 | async-start | bytes 10485760 | tf_op jit(solution)/shard_map/all_gather | solution.py:8
  9.1 280.7 %reduce-scatter.2.cloned.1.call-start = ((), (), s32[]{:S(2)}) async-start(), calls=%async_computation.4 | async-start | bytes 10485760 | tf_op jit(solution)/shard_map/reduce_scatter | solution.py:14
Sparse Core Ops, SparseCore 0:
  9.8 78.4 all-gather.2
  90.1 85.4 all-gather.4
  206.8 82.9 reduce-scatter.1
where the time goes:
time: 360 us
  waiting for transfers between devices  244 us (68%)
  blocking collectives  59.5 us (17%)
  matrix products  31 us (9%)
  between operations  13.1 us (4%)
  local copies, waits for them, and re-layouts  12.8 us (4%)
    reduce_scatter x1, waiting for transfers between devices, shards(): lax.psum_scatter(lax.dot_general(flat_panel, rows_w, (((0,), (1,)), ((),...  83.1 us
    all_gather x1, waiting for transfers between devices, shards(): rows_w = lax.all_gather(integrals, 'col', axis=0, tiled=True)  80.8 us
    all_gather x1, waiting for transfers between devices, shards(): panel_t = lax.all_gather(amplitudes, 'row', axis=2, tiled=True)  79.2 us
    all_to_all x1, blocking collectives, shards(): lax.all_to_all(shares, 'row', split_axis=2, concat_axis=3, tiled=True)  59.5 us
    dot_general x1, matrix products, shards(): lax.dot_general(flat_panel, rows_w, (((0,), (1,)), ((), ())), precision=l...  31 us
  transfers between devices with their start and end apart: 3, of which 3 were waited for; matrix products, arithmetic and copies ran while one was open for 2% of the time, Pallas kernels for 0%

commit v1 on v0

--- a/solution.py
+++ b/solution.py
@@ -6,7 +6,9 @@
 
 def shards(integrals, amplitudes):
     rows_w = lax.all_gather(integrals, "col", axis=0, tiled=True)
-    panel_t = lax.all_gather(amplitudes, "row", axis=2, tiled=True)
+    panel_t = jnp.concatenate(
+        lax.all_to_all(jnp.stack([amplitudes] * lax.axis_size("row")), "row", 0, 0), axis=2
+    )
     kc_rows, i_count, j_count = panel_t.shape
     flat_panel = panel_t.reshape(kc_rows, i_count * j_count)
     row_count = lax.axis_size("row")

time: 360 us -> 366 us (1.017)
  blocking collectives: 59.5 us -> 205 us
  waiting for transfers between devices: 244 us -> 102 us
    all_to_all x0 -> x1, blocking collectives: none -> 146 us  [shards(): lax.all_to_all(jnp.stack([amplitudes] * lax.axis_size('row')), 'row', 0, 0)]
    all_gather x1 -> x0, waiting for transfers between devices: 79.2 us -> none  [shards(): panel_t = lax.all_gather(amplitudes, 'row', axis=2, tiled=True)]
    all_gather x1, waiting for transfers between devices: 80.8 us -> 17.2 us  [shards(): rows_w = lax.all_gather(integrals, 'col', axis=0, tiled=True)]
    another operation x0 -> x2, local copies, waits for them, and re-layouts: none -> 7.29 us  [the longest x1 5.29 us: shards(): flat_panel = panel_t.reshape(kc_rows, i_count * j_count)]
    all_gather x1 -> x0, local copies, waits for them, and re-layouts: 6.55 us -> none  [shards(): panel_t = lax.all_gather(amplitudes, 'row', axis=2, tiled=True)]
  transfers between devices with their start and end apart: 3 -> 2, of which waited for: 3 -> 2; matrix products, arithmetic and copies ran while one was open for 2% -> 3% of each run, Pallas kernels for 0% -> 0%
where the time goes in v1:
time: 366 us
  blocking collectives  205 us (56%)
  waiting for transfers between devices  102 us (28%)
  matrix products  31 us (8%)
  local copies, waits for them, and re-layouts  14.6 us (4%)
  between operations  13.4 us (4%)
    all_to_all x1, blocking collectives, shards(): lax.all_to_all(jnp.stack([amplitudes] * lax.axis_size('row')), 'row', 0, 0)  146 us
    reduce_scatter x1, waiting for transfers between devices, shards(): lax.psum_scatter(lax.dot_general(flat_panel, rows_w, (((0,), (1,)), ((),...  83.9 us
    all_to_all x1, blocking collectives, shards(): lax.all_to_all(shares, 'row', split_axis=2, concat_axis=3, tiled=True)  59.6 us
    dot_general x1, matrix products, shards(): lax.dot_general(flat_panel, rows_w, (((0,), (1,)), ((), ())), precision=l...  31 us
    all_gather x1, waiting for transfers between devices, shards(): rows_w = lax.all_gather(integrals, 'col', axis=0, tiled=True)  17.2 us
  transfers between devices with their start and end apart: 2, of which 2 were waited for; matrix products, arithmetic and copies ran while one was open for 3% of the time, Pallas kernels for 0%

profile of v1, /device:TPU:1, one launch (start us, length us, event | category | flops | bytes accessed | tf_op | source)
XLA Modules:
  0.0 366.0 jit_solution(14342369186821219579)
XLA Ops:
  6.5 0.0 all-gather.2.cloned.1.call-start
  6.5 0.7 all-gather.2.cloned.1.call-update
  7.3 0.0 reduce-scatter.2.cloned.1.call-start
  7.3 2.0 stack.2
  9.3 145.7 %all_to_all.14 = f32[16,1024,16,4]{1,3,2,0:T(4,128)S(1)} all-to-all(f32[16,1024,16,4]{1,3,2,0:T(4,128)S(1)} %stack.2), channel_id=1, replica_groups=mesh['row'=16,'col'=4,'depth'=4] {'row'}, dimensions={0} | all-to-all | bytes 8388608 | tf_op jit(solution)/shard_map/all_to_all | solution.py:10
  155.0 2.9 copy.6
  157.9 5.3 %reshape_reshape.3 = f32[1024,1024]{0,1:T(8,128)} reshape(f32[1024,16,16,4]{0,3,2,1:T(4,128)} %copy.6) | data formatting | bytes 8388608 | tf_op jit(solution)/shard_map/reshape;reshape | solution.py:13
  163.2 17.2 %all-gather.2.cloned.1.call-done = f32[2048,1024]{1,0:T(8,128)} async-done(((f32[512,1024]{1,0:T(8,128)}), f32[2048,1024]{1,0:T(8,128)}) %all-gather.2.cloned.1.call-update) | async-done | bytes 8388624 | tf_op jit(solution)/shard_map/all_gather | solution.py:8
  180.3 31.0 %fusion = f32[1024,2048]{1,0:T(8,128)} fusion(f32[1024,1024]{0,1:T(8,128)} %reshape_reshape.3, f32[2048,1024]{1,0:T(8,128)} %all-gather.2.cloned.1.call-done), kind=kOutput, calls=%fused_computation | convolution fusion | flops 25769803776 | bytes 20971520 | tf_op jit(solution)/shard_map/dot_general | solution.py:17
  211.3 0.0 reduce-scatter.2.cloned.1.call-update
  211.4 83.9 %reduce-scatter.2.cloned.1.call-done = f32[256,2048]{1,0:T(8,128)} async-done(((f32[1024,2048]{1,0:T(8,128)}), f32[256,2048]{1,0:T(8,128)}) %reduce-scatter.2.cloned.1.call-update) | async-done | bytes 2097168 | tf_op jit(solution)/shard_map/reduce_scatter | solution.py:16
  295.2 2.9 copy.7
  298.2 59.6 %all_to_all.15 = f32[4,4,16,2048]{3,1,0,2:T(4,128)S(1)} all-to-all(f32[4,4,16,2048]{3,1,0,2:T(4,128)S(1)} %copy.7), channel_id=1, replica_groups=mesh['row'=16,'col'=4,'depth'=4] {'row'}, dimensions={2} | all-to-all | bytes 4194304 | tf_op jit(solution)/shard_map/all_to_all | solution.py:29
  357.7 1.5 copy.9
Async XLA Ops:
  6.5 173.8 %all-gather.2.cloned.1.call-start = ((), (), s32[]{:S(2)}) async-start(), calls=%async_computation.3 | async-start | bytes 10485760 | tf_op jit(solution)/shard_map/all_gather | solution.py:8
  7.3 288.0 %reduce-scatter.2.cloned.1.call-start = ((), (), s32[]{:S(2)}) async-start(), calls=%async_computation.4 | async-start | bytes 10485760 | tf_op jit(solution)/shard_map/reduce_scatter | solution.py:16
Sparse Core Ops, SparseCore 0:
  9.2 171.1 all-gather.1
  211.5 83.6 reduce-scatter.1
